TPU v7x, 32 devices: a whole 2x2x4 slice. The times are simulated.
32 devices in a mesh: ctx: 4 (over z), tp: 8 (over y, x, core).
Axes of the slice: x: 2, y: 2, z: 4, core: 2. Of those that a mesh axis runs over, the one named last changes fastest.
Arguments:
- queries: bfloat16 [2048, 4096], P('ctx', 'tp'), may hold values from -15 to 15
- keys: bfloat16 [2048, 1024], P('ctx', 'tp'), may hold values from -15 to 15, as said below
- values: bfloat16 [2048, 1024], P('ctx', 'tp'), may hold values from -6 to 6, as said below
- doc_blocks: int32 [16], replicated, may hold values from 0 to 5, never falling along the last dimension, each value on 1 to 8 neighbouring positions
Outputs:
- attended: bfloat16 [2048, 4096], P('ctx', 'tp')
Inputs may be any that keep to these rules, and one draw needn't show every extreme that they name: `doc_blocks`: ids never fall along the row; each document covers 1 to 8 blocks and one covers exactly that many. `keys`: copies of the same key-value head are equal. `values`: copies of the same key-value head are equal.
All inputs are finite; a program needn't handle non-finite values.
Results may differ from a plain program's by a relative error of at most 0.0047.
Values may be sent and summed in bfloat16 or wider, within the bound.
No kernel may reach another device: no remote copies, remote signals or barrier semaphores. Data moves between devices by JAX's collectives and lax.ppermute only.
A program may use at most 64 MiB of HBM per device.

v0:
```python
import jax
import jax.numpy as jnp
from jax import lax
from jax.sharding import PartitionSpec as P

HD = 128
BLK = 128


def positions(rows, span_rows, shards):
    stored_block = rows // span_rows
    half_index = stored_block // 2
    span = jnp.where(stored_block % 2 == 0, half_index, 2 * shards - 1 - half_index)
    return span * span_rows + rows % span_rows


def block_scores(query_block, key_part, query_pos, query_doc, key_pos, key_doc):
    scores = jnp.einsum(
        "qgrd,kgd->grqk", query_block, key_part, preferred_element_type=jnp.float32
    ) * HD ** (-0.5)
    allowed = (query_doc[:, None] == key_doc[None, :]) & (key_pos[None, :] <= query_pos[:, None])
    return (jnp.where(allowed, scores, -1e30), allowed)


def body(queries, keys, values, doc_blocks):
    span_rows = queries.shape[0] // 2
    shards = lax.axis_size("ctx")
    shard = lax.axis_index("ctx")
    heads_here = queries.shape[1] // HD
    kv_heads = keys.shape[1] // HD
    repeat_count = heads_here // kv_heads
    query_block = min(span_rows, 128)
    block_count = 2 * span_rows // query_block
    local_rows = shard * 2 * span_rows + jnp.arange(2 * span_rows, dtype=jnp.int32)
    query_pos = positions(local_rows, span_rows, shards)
    query_doc = doc_blocks[query_pos // BLK]
    query_blocks = queries.reshape(block_count, query_block, kv_heads, repeat_count, HD)
    pos_blocks = query_pos.reshape(block_count, query_block)
    doc_query_blocks = query_doc.reshape(block_count, query_block)
    whole_keys, whole_values = (
        lax.all_gather(keys, "ctx", axis=0, tiled=True),
        lax.all_gather(values, "ctx", axis=0, tiled=True),
    )
    piece_key_pos = positions(jnp.arange(whole_keys.shape[0], dtype=jnp.int32), span_rows, shards)
    key_doc = doc_blocks[piece_key_pos // BLK]
    key_part = whole_keys.reshape(-1, kv_heads, HD)
    value_part = whole_values.reshape(-1, kv_heads, HD)

    def one_block(item):
        block, block_pos, block_doc = item
        scores, allowed = block_scores(
            block, key_part, block_pos, block_doc, piece_key_pos, key_doc
        )
        peak_value = jnp.max(scores, axis=-1, keepdims=True)
        weight = jnp.where(allowed, jnp.exp(scores - peak_value), 0.0)
        total = jnp.sum(weight, axis=-1, keepdims=True)
        probs = (weight / total).astype(jnp.bfloat16)
        return jnp.einsum("grqk,kgd->qgrd", probs, value_part, preferred_element_type=jnp.float32)

    mixed = lax.map(one_block, (query_blocks, pos_blocks, doc_query_blocks))
    return mixed.reshape(2 * span_rows, heads_here * HD).astype(jnp.bfloat16)


def solution(mesh):
    return jax.shard_map(
        body,
        mesh=mesh,
        in_specs=(P("ctx", "tp"), P("ctx", "tp"), P("ctx", "tp"), P()),
        out_specs=P("ctx", "tp"),
        check_vma=False,
    )
```

profile of v0, /device:TPU:0, one launch (start us, length us, event | category | flops | bytes accessed | tf_op | source)
XLA Modules:
  0.0 76.9 jit_solution(50103550590367720)
XLA Ops:
  0.0 2.0 %fusion.44 = (s32[1]{0:T(128)}, s32[1]{0:T(128)}, s32[1]{0:T(128)}, s32[1]{0:T(128)}, s32[1]{0:T(128)}, /*index=5*/s32[1]{0:T(128)}, s32[1]{0:T(128)}, s32[1]{0:...) fusion(s32[16]{0:T(128)} %param.9), kind=kLoop, calls=%fused_computation.136 | loop fusion | bytes 128 | tf_op jit(solution)/shard_map/gather | solution.py:36
  2.0 4.4 %compare_select_fusion.15 = s32[512,1]{0,1:T(1,128)S(1)} fusion(s32[]{:T(128)} %bitcast.9, s32[]{:T(128)} %bitcast.10, s32[]{:T(128)} %bitcast.11, s32[]{:T(128)} %bitcast.12, s32[]{:T(128)} %bitcast.13, s32[]{:T(128)} %bitcast.15, s32[]{:T(128)} %bitcast.14, s32[]{:T(128)S(6)} %mul.43), kind=kLoop, calls=%fused_computation.92 | loop fusion | flops 37888 | bytes 2080 | tf_op jit(solution)/shard_map/gather | solution.py:36
  6.8 5.6 %select_bitcast_fusion = s32[4,128]{1,0:T(4,128)S(1)} fusion(pred[512]{0:T(512)(128)(4,1)S(1)} %get-tuple-element.115, pred[512]{0:T(512)(128)(4,1)S(1)} %get-tuple-element.116, pred[512]{0:T(512)(128)(4,1)S(1)} %get-tuple-element.117, pred[512]{0:T(512)(128)(4,1)S(1)} %get-tuple-element.118, pred[512]{0:T(512)(128)(4,1)S(1)} %get-tuple-element.119, ...), kind=kLoop, calls=%fused_computation.128 | loop fusion | flops 4608 | bytes 8740 | tf_op jit(solution)/shard_map/reshape | solution.py:39
  12.4 4.5 %compare_select_fusion.1 = s32[2048,1]{0,1:T(1,128)S(1)} fusion(s32[]{:T(128)} %bitcast.9, s32[]{:T(128)} %bitcast.10, s32[]{:T(128)} %bitcast.11, s32[]{:T(128)} %bitcast.12, s32[]{:T(128)} %bitcast.13, s32[]{:T(128)} %bitcast.15, s32[]{:T(128)} %bitcast.14), kind=kLoop, calls=%fused_computation.59 | loop fusion | flops 135168 | bytes 8220 | tf_op jit(solution)/shard_map/gather | solution.py:45
  16.8 0.1 compare_reduce_fusion
  16.9 0.1 compare_reduce_fusion.1
  17.1 0.1 compare_reduce_fusion.2
  17.3 0.1 compare_reduce_fusion.4
  17.4 0.1 compare_reduce_fusion.5
  17.9 5.6 %select_select_fusion = s32[2048]{0:T(1024)S(1)} fusion(pred[2048]{0:T(1024)(128)(4,1)S(1)} %compare_reduce_fusion, pred[2048]{0:T(1024)(128)(4,1)S(1)} %compare_reduce_fusion.1, pred[2048]{0:T(1024)(128)(4,1)S(1)} %compare_reduce_fusion.2, pred[2048]{0:T(1024)(128)(4,1)S(1)} %compare_reduce_fusion.3, pred[2048]{0:T(1024)(128)(4,1)S(1)} %compare_reduce_fusion.4, ...), kind=kLoop, calls=%fused_computation.82 | loop fusion | flops 18432 | bytes 34852 | tf_op jit(solution)/shard_map/gather | solution.py:45
  23.5 17.6 %all_gather.6 = bf16[2048,128]{1,0:T(8,128)(2,1)S(1)} all-gather(bf16[512,128]{1,0:T(8,128)(2,1)} %param.7), channel_id=1, replica_groups=mesh['ctx'=4,'tp'=8] {'ctx'}, dimensions={0}, use_global_device_ids=true | all-gather | bytes 655360 | tf_op jit(solution)/shard_map/all_gather | solution.py:41
  41.1 16.6 %all_gather.7 = bf16[2048,128]{1,0:T(8,128)(2,1)S(1)} all-gather(bf16[512,128]{1,0:T(8,128)(2,1)} %param.8), channel_id=1, replica_groups=mesh['ctx'=4,'tp'=8] {'ctx'}, dimensions={0}, use_global_device_ids=true | all-gather | bytes 655360 | tf_op jit(solution)/shard_map/all_gather | solution.py:42
  57.6 1.2 %reshape.436 = bf16[4,128,1,4,128]{4,3,1,0,2:T(4,128)(2,1)S(1)} reshape(bf16[512,512]{1,0:T(8,128)(2,1)} %param.6) | data formatting | bytes 1048576 | tf_op jit(solution)/shard_map/reshape | solution.py:37
  58.8 16.8 %while.11 = (s32[]{:T(128)}, bf16[4,128,1,4,128]{4,1,3,2,0:T(8,128)(2,1)S(1)}, s32[4,128]{1,0:T(4,128)S(1)}, s32[2048]{0:T(1024)S(1)}, s32[4,128]{1,0:T(4,128)S(...) while((s32[]{:T(128)}, ...), condition=%wide.region_3.4_spmd.clone, body=%wide.region_0.3_spmd.clone.sunk | while | flops 552410112 | bytes 15373417 | solution.py:60
  58.8 0.3 compare_and_fusion.2
  59.2 1.0 %fusion.56 = (f32[4,128]{1,0:T(4,128)S(1)}, f32[128,4,2048]{2,0,1:T(8,128)S(1)}) fusion(pred[128,2048]{1,0:T(8,128)(4,1)S(1)} %compare_and_fusion.2, bf16[2048,1,128]{2,0,1:T(8,128)(2,1)S(1)} %get-tuple-element.204, bf16[1,128,1,4,128]{4,3,1,0,2:T(4,128)(2,1)S(1)} %constant_dynamic-slice_fusion.4), kind=kOutput, calls=%fused_computation.4.clone.1 | convolution fusion | flops 271580672 | bytes 5113856 | tf_op jit(solution)/shard_map/while/body/eval_jaxpr/qgrd,kgd->grqk/dot_general | solution.py:18
  60.2 1.3 %fusion.57 = f32[4,128]{1,0:T(4,128)S(1)} fusion(f32[128,4,2048]{2,0,1:T(8,128)S(1)} %get-tuple-element.178, f32[4,128]{1,0:T(4,128)S(1)} %get-tuple-element.179, pred[128,2048]{1,0:T(8,128)(4,1)S(1)} %compare_and_fusion.2), kind=kLoop, calls=%fused_computation.5.clone.1 | loop fusion | flops 5242368 | bytes 4460544 | tf_op jit(solution)/shard_map/while/body/eval_jaxpr/reduce_sum | solution.py:56
  61.5 1.5 %fusion.58 = bf16[4,128,1,4,128]{4,1,3,2,0:T(8,128)(2,1)S(1)} fusion(bf16[4,128,1,4,128]{4,1,3,2,0:T(8,128)(2,1)S(1)} %get-tuple-element.190, s32[]{:T(128)} %get-tuple-element.189, f32[4,128]{1,0:T(4,128)S(1)} %fusion.57, f32[4,128]{1,0:T(4,128)S(1)} %get-tuple-element.179, f32[128,4,2048]{2,0,1:T(8,128)S(1)} %get-tuple-element.178, ...), kind=kOutput, calls=%fused_computation.9.clone.1 | convolution fusion | flops 274726912 | bytes 5246980 | tf_op jit(solution)/shard_map/while/body/eval_jaxpr/grqk,kgd->qgrd/dot_general | solution.py:58
  63.0 0.3 compare_and_fusion.2
  63.4 1.0 %fusion.56 = (f32[4,128]{1,0:T(4,128)S(1)}, f32[128,4,2048]{2,0,1:T(8,128)S(1)}) fusion(pred[128,2048]{1,0:T(8,128)(4,1)S(1)} %compare_and_fusion.2, bf16[2048,1,128]{2,0,1:T(8,128)(2,1)S(1)} %get-tuple-element.204, bf16[1,128,1,4,128]{4,3,1,0,2:T(4,128)(2,1)S(1)} %constant_dynamic-slice_fusion.4), kind=kOutput, calls=%fused_computation.4.clone.1 | convolution fusion | flops 271580672 | bytes 5113856 | tf_op jit(solution)/shard_map/while/body/eval_jaxpr/qgrd,kgd->grqk/dot_general | solution.py:18
  64.4 1.3 %fusion.57 = f32[4,128]{1,0:T(4,128)S(1)} fusion(f32[128,4,2048]{2,0,1:T(8,128)S(1)} %get-tuple-element.178, f32[4,128]{1,0:T(4,128)S(1)} %get-tuple-element.179, pred[128,2048]{1,0:T(8,128)(4,1)S(1)} %compare_and_fusion.2), kind=kLoop, calls=%fused_computation.5.clone.1 | loop fusion | flops 5242368 | bytes 4460544 | tf_op jit(solution)/shard_map/while/body/eval_jaxpr/reduce_sum | solution.py:56
  65.7 1.5 %fusion.58 = bf16[4,128,1,4,128]{4,1,3,2,0:T(8,128)(2,1)S(1)} fusion(bf16[4,128,1,4,128]{4,1,3,2,0:T(8,128)(2,1)S(1)} %get-tuple-element.190, s32[]{:T(128)} %get-tuple-element.189, f32[4,128]{1,0:T(4,128)S(1)} %fusion.57, f32[4,128]{1,0:T(4,128)S(1)} %get-tuple-element.179, f32[128,4,2048]{2,0,1:T(8,128)S(1)} %get-tuple-element.178, ...), kind=kOutput, calls=%fused_computation.9.clone.1 | convolution fusion | flops 274726912 | bytes 5246980 | tf_op jit(solution)/shard_map/while/body/eval_jaxpr/grqk,kgd->qgrd/dot_general | solution.py:58
  67.2 0.3 compare_and_fusion.2
  67.6 1.0 %fusion.56 = (f32[4,128]{1,0:T(4,128)S(1)}, f32[128,4,2048]{2,0,1:T(8,128)S(1)}) fusion(pred[128,2048]{1,0:T(8,128)(4,1)S(1)} %compare_and_fusion.2, bf16[2048,1,128]{2,0,1:T(8,128)(2,1)S(1)} %get-tuple-element.204, bf16[1,128,1,4,128]{4,3,1,0,2:T(4,128)(2,1)S(1)} %constant_dynamic-slice_fusion.4), kind=kOutput, calls=%fused_computation.4.clone.1 | convolution fusion | flops 271580672 | bytes 5113856 | tf_op jit(solution)/shard_map/while/body/eval_jaxpr/qgrd,kgd->grqk/dot_general | solution.py:18
  68.6 1.3 %fusion.57 = f32[4,128]{1,0:T(4,128)S(1)} fusion(f32[128,4,2048]{2,0,1:T(8,128)S(1)} %get-tuple-element.178, f32[4,128]{1,0:T(4,128)S(1)} %get-tuple-element.179, pred[128,2048]{1,0:T(8,128)(4,1)S(1)} %compare_and_fusion.2), kind=kLoop, calls=%fused_computation.5.clone.1 | loop fusion | flops 5242368 | bytes 4460544 | tf_op jit(solution)/shard_map/while/body/eval_jaxpr/reduce_sum | solution.py:56
  69.8 1.5 %fusion.58 = bf16[4,128,1,4,128]{4,1,3,2,0:T(8,128)(2,1)S(1)} fusion(bf16[4,128,1,4,128]{4,1,3,2,0:T(8,128)(2,1)S(1)} %get-tuple-element.190, s32[]{:T(128)} %get-tuple-element.189, f32[4,128]{1,0:T(4,128)S(1)} %fusion.57, f32[4,128]{1,0:T(4,128)S(1)} %get-tuple-element.179, f32[128,4,2048]{2,0,1:T(8,128)S(1)} %get-tuple-element.178, ...), kind=kOutput, calls=%fused_computation.9.clone.1 | convolution fusion | flops 274726912 | bytes 5246980 | tf_op jit(solution)/shard_map/while/body/eval_jaxpr/grqk,kgd->qgrd/dot_general | solution.py:58
  71.4 0.3 compare_and_fusion.2
  71.8 1.0 %fusion.56 = (f32[4,128]{1,0:T(4,128)S(1)}, f32[128,4,2048]{2,0,1:T(8,128)S(1)}) fusion(pred[128,2048]{1,0:T(8,128)(4,1)S(1)} %compare_and_fusion.2, bf16[2048,1,128]{2,0,1:T(8,128)(2,1)S(1)} %get-tuple-element.204, bf16[1,128,1,4,128]{4,3,1,0,2:T(4,128)(2,1)S(1)} %constant_dynamic-slice_fusion.4), kind=kOutput, calls=%fused_computation.4.clone.1 | convolution fusion | flops 271580672 | bytes 5113856 | tf_op jit(solution)/shard_map/while/body/eval_jaxpr/qgrd,kgd->grqk/dot_general | solution.py:18
  72.8 1.3 %fusion.57 = f32[4,128]{1,0:T(4,128)S(1)} fusion(f32[128,4,2048]{2,0,1:T(8,128)S(1)} %get-tuple-element.178, f32[4,128]{1,0:T(4,128)S(1)} %get-tuple-element.179, pred[128,2048]{1,0:T(8,128)(4,1)S(1)} %compare_and_fusion.2), kind=kLoop, calls=%fused_computation.5.clone.1 | loop fusion | flops 5242368 | bytes 4460544 | tf_op jit(solution)/shard_map/while/body/eval_jaxpr/reduce_sum | solution.py:56
  74.0 1.5 %fusion.58 = bf16[4,128,1,4,128]{4,1,3,2,0:T(8,128)(2,1)S(1)} fusion(bf16[4,128,1,4,128]{4,1,3,2,0:T(8,128)(2,1)S(1)} %get-tuple-element.190, s32[]{:T(128)} %get-tuple-element.189, f32[4,128]{1,0:T(4,128)S(1)} %fusion.57, f32[4,128]{1,0:T(4,128)S(1)} %get-tuple-element.179, f32[128,4,2048]{2,0,1:T(8,128)S(1)} %get-tuple-element.178, ...), kind=kOutput, calls=%fused_computation.9.clone.1 | convolution fusion | flops 274726912 | bytes 5246980 | tf_op jit(solution)/shard_map/while/body/eval_jaxpr/grqk,kgd->qgrd/dot_general | solution.py:58
  75.6 0.4 copy.7
  76.0 0.9 %copy.15 = bf16[64,8,4,128]{3,1,2,0:T(8,128)(2,1)} copy(bf16[64,8,4,128]{3,2,1,0:T(4,128)(2,1)S(1)} %bitcast.104) | data formatting | bytes 1048576
  (23 shorter events, 1.2 us)
where the time goes:
time: 77.3 us; the launch traced here: 76.9 us
  blocking collectives  34.1 us (44%)
  other arithmetic  27.7 us (36%)
  matrix products  10.1 us (13%)
  local copies, waits for them, and re-layouts  4.65 us (6%)
    all_gather x1, blocking collectives, body(): lax.all_gather(keys, 'ctx', axis=0, tiled=True)  17.6 us
    all_gather x1, blocking collectives, body(): lax.all_gather(values, 'ctx', axis=0, tiled=True)  16.6 us
    gather x11, other arithmetic, body(): key_doc = doc_blocks[piece_key_pos // BLK]  11.1 us
    dot_general x4, matrix products, one_block(): jnp.einsum('grqk,kgd->qgrd', probs, value_part, preferred_element_type=jn...  6.07 us
    reshape x1, other arithmetic, body(): doc_query_blocks = query_doc.reshape(block_count, query_block)  5.59 us
    reduce_sum x4, other arithmetic, one_block(): total = jnp.sum(weight, axis=-1, keepdims=True)  5.05 us
    gather x6, other arithmetic, body(): query_doc = doc_blocks[query_pos // BLK]  4.8 us
    dot_general x4, matrix products, block_scores(): jnp.einsum('qgrd,kgd->grqk', query_block, key_part, preferred_element_typ...  4.04 us

commit v1 on v0

v1 whole, which is shorter than its diff:
```python
import math

import jax
import jax.numpy as jnp
from jax import lax
from jax.experimental import pallas as pl
from jax.experimental.pallas import tpu as pltpu
from jax.sharding import PartitionSpec as P

HD = 128
BLK = 128
MASKED = -1e30
SCALE2 = HD ** (-0.5) * math.log2(math.e)
VMEM = pl.BlockSpec(memory_space=pltpu.VMEM)
SMEM = pl.BlockSpec(memory_space=pltpu.SMEM)


def pack_kernel(shards, k_ref, v_ref, doc_ref, both_ref, *refs):
    sends, plan_ref = refs[:-1], refs[-1]
    me = lax.axis_index("ctx")
    span = k_ref.shape[0] // 2
    per_span = span // BLK
    for r, send in enumerate(sends, 1):
        row = pl.multiple_of(jnp.where((me ^ r) > me, 0, span), span)
        send[:span, :] = k_ref[pl.ds(row, span), :]
        send[span:, :] = v_ref[pl.ds(row, span), :]
    both_ref[: 2 * span, :] = k_ref[...]
    both_ref[2 * span :, :] = v_ref[...]
    wide = jnp.int32(0)
    for s in range(1, shards):
        last = doc_ref[per_span * (s + 1) - 1]
        first = doc_ref[per_span * (2 * shards - s)]
        wide = jnp.where(last == first, 1, wide)
    plan_ref[0] = wide


def attend_kernel(shards, sources, q_ref, k_ref, v_ref, doc_ref, *refs):
    received, (o_ref, m_ref, acc_ref) = refs[:-3], refs[-3:]
    me = lax.axis_index("ctx")
    span = k_ref.shape[0] // 2
    per_span = span // BLK
    chunk = min(span, 2 * BLK)
    blocks = chunk // BLK
    chunks = span // chunk
    heads = q_ref.shape[1] // HD
    spans = (me, 2 * shards - 1 - me)
    row_in = lax.broadcasted_iota(jnp.int32, (BLK, BLK), 0)
    col_in = lax.broadcasted_iota(jnp.int32, (BLK, BLK), 1)
    triangle = jnp.where(col_in <= row_in, 0.0, MASKED).astype(jnp.float32)
    ones = jnp.ones((chunk, HD), jnp.bfloat16)

    def tile(t, query_chunk, key_chunk, source, key_span, diagonal, first):
        keys, key_row, values, value_row = source
        query_row = t * span + query_chunk * chunk
        key_rows = pl.ds(pl.multiple_of(key_row + key_chunk * chunk, BLK), chunk)
        value_rows = pl.ds(pl.multiple_of(value_row + key_chunk * chunk, BLK), chunk)
        rows = pl.ds(pl.multiple_of(query_row, BLK), chunk)
        query_block = spans[t] * per_span + query_chunk * blocks
        key_block = key_span * per_span + key_chunk * blocks
        bias = {}
        for a in range(blocks):
            for c in range(blocks):
                same = doc_ref[query_block + a] == doc_ref[key_block + c]
                if diagonal and c > a:
                    same = jnp.bool_(False)
                bias[a, c] = jnp.where(same, 0.0, MASKED).astype(jnp.float32)
        key = keys[key_rows, :]
        value = jnp.concatenate([values[value_rows, :], ones], axis=1)
        for h in range(heads):
            query = q_ref[rows, h * HD : (h + 1) * HD]
            scores = lax.dot_general(
                query, key, (((1,), (1,)), ((), ())), preferred_element_type=jnp.float32
            )
            parts = []
            for a in range(blocks):
                line = []
                for c in range(blocks):
                    part = scores[a * BLK : (a + 1) * BLK, c * BLK : (c + 1) * BLK]
                    part = part + bias[a, c]
                    if diagonal and a == c:
                        part = part + triangle
                    line.append(part)
                parts.append(line)
            peak = jnp.concatenate(
                [
                    jnp.broadcast_to(
                        jnp.max(
                            line[0] if blocks == 1 else jnp.maximum(*line),
                            axis=1,
                            keepdims=True,
                        ),
                        (BLK, HD),
                    )
                    for line in parts
                ],
                axis=0,
            )
            if not first:
                before = m_ref[h, rows, :]
                peak = jnp.maximum(peak, before)
            weights = jnp.concatenate(
                [
                    jnp.concatenate(
                        [
                            jnp.exp2((part - peak[a * BLK : (a + 1) * BLK]) * SCALE2)
                            for part in line
                        ],
                        axis=1,
                    )
                    for a, line in enumerate(parts)
                ],
                axis=0,
            ).astype(jnp.bfloat16)
            mixed = jnp.dot(weights, value, preferred_element_type=jnp.float32)
            if not first:
                shrink = jnp.exp2((before - peak) * SCALE2)
                mixed = mixed + acc_ref[h, rows, :] * jnp.concatenate([shrink, shrink], axis=1)
            m_ref[h, rows, :] = peak
            acc_ref[h, rows, :] = mixed

    def needed(t, query_chunk, key_chunk, key_span):
        last = doc_ref[key_span * per_span + (key_chunk + 1) * blocks - 1]
        first = doc_ref[spans[t] * per_span + query_chunk * blocks]
        return last == first

    def whole_span(t, source, key_span, earlier):
        def step(index, carry):
            query_chunk, key_chunk = index // chunks, index % chunks

            @pl.when(earlier & needed(t, query_chunk, key_chunk, key_span))
            def _():
                tile(t, query_chunk, key_chunk, source, key_span, False, False)

            return carry

        lax.fori_loop(0, chunks * chunks, step, 0)

    own = [(k_ref, 0, v_ref, 0), (k_ref, span, v_ref, span)]
    for t in range(2):

        def diagonal_step(index, carry):
            tile(t, index, index, own[t], spans[t], True, True)

            def before_step(key_chunk, inner):
                @pl.when(needed(t, index, key_chunk, spans[t]))
                def _():
                    tile(t, index, key_chunk, own[t], spans[t], False, False)

                return inner

            if chunks > 1:
                lax.fori_loop(0, index, before_step, 0)
            return carry

        lax.fori_loop(0, chunks, diagonal_step, 0)
    if sources == "gathered":
        all_keys, all_values = received
        for t in range(2):

            def span_step(s, carry, t=t):
                holder = jnp.minimum(s, 2 * shards - 1 - s)
                row = (2 * holder + jnp.where(s < shards, 0, 1)) * span
                whole_span(t, (all_keys, row, all_values, row), s, jnp.bool_(True))
                return carry

            lax.fori_loop(0, spans[t], span_step, 0)
        sources = []
    else:
        whole_span(1, own[0], spans[0], jnp.bool_(True))
    for r, kind in sources:
        ref = received[r - 1]
        partner = me ^ r
        if kind == "one":
            key_span = jnp.where(partner < me, partner, 2 * shards - 1 - partner)
            found = [((ref, 0, ref, span), key_span)]
        else:
            found = [
                ((ref, 0, ref, 2 * span), partner),
                ((ref, span, ref, 3 * span), 2 * shards - 1 - partner),
            ]
        for source, key_span in found:
            for t in range(2):
                whole_span(t, source, key_span, key_span < spans[t])

    for h in range(heads):
        total = acc_ref[h, :, HD:]
        o_ref[:, h * HD : (h + 1) * HD] = (acc_ref[h, :, :HD] / total).astype(jnp.bfloat16)


def body(queries, keys, values, doc_blocks):
    shards = lax.axis_size("ctx")
    rows, heads = queries.shape[0], queries.shape[1] // HD
    span = rows // 2
    send_shape = jax.ShapeDtypeStruct((2 * span, HD), jnp.bfloat16)
    both_shape = jax.ShapeDtypeStruct((4 * span, HD), jnp.bfloat16)
    partners = range(1, shards)

    def attend(sources, received):
        return pl.pallas_call(
            lambda *refs: attend_kernel(shards, sources, *refs),
            in_specs=[VMEM, VMEM, VMEM, SMEM] + [VMEM] * len(received),
            out_specs=VMEM,
            out_shape=jax.ShapeDtypeStruct(queries.shape, jnp.bfloat16),
            scratch_shapes=[
                pltpu.VMEM((heads, rows, HD), jnp.float32),
                pltpu.VMEM((heads, rows, 2 * HD), jnp.float32),
            ],
            compiler_params=pltpu.CompilerParams(vmem_limit_bytes=48 * 1024 * 1024),
            name="attend",
        )(queries, keys, values, doc_blocks, *received)

    if shards != 4:
        received = [lax.all_gather(x, "ctx", axis=0, tiled=True) for x in (keys, values)]
        return attend("gathered", received)

    both, *sends, plan = pl.pallas_call(
        lambda *refs: pack_kernel(shards, *refs),
        in_specs=[VMEM, VMEM, SMEM],
        out_specs=[VMEM] * shards + [SMEM],
        out_shape=[both_shape]
        + [send_shape] * (shards - 1)
        + [jax.ShapeDtypeStruct((1,), jnp.int32)],
        name="pack",
    )(keys, values, doc_blocks)

    def swap(array, r):
        return lax.ppermute(array, "ctx", [(i, i ^ r) for i in range(shards)])

    def narrow(_):
        received = [swap(sends[r - 1], r) for r in partners]
        return attend([(r, "one") for r in partners], received)

    def wide(_):
        received = [swap(both, r) for r in partners]
        return attend([(r, "two") for r in partners], received)

    return lax.switch(plan[0], [narrow, wide], 0)


def solution(mesh):
    return jax.shard_map(
        body,
        mesh=mesh,
        in_specs=(P("ctx", "tp"), P("ctx", "tp"), P("ctx", "tp"), P()),
        out_specs=P("ctx", "tp"),
        check_vma=False,
    )
```

time: 77.3 us -> 33.7 us (0.44)
  blocking collectives: 34.1 us -> 0 us
  other arithmetic: 27.7 us -> 0 us
  waiting for transfers between devices: 0 us -> 21.7 us
  matrix products: 10.1 us -> 0 us
  starting transfers between devices: 0 us -> 5.62 us
  Pallas kernels: 0 us -> 3.75 us
  local copies, waits for them, and re-layouts: 4.65 us -> 1.43 us
    all_gather x2 -> x0, blocking collectives: 34.1 us -> none  [the longest x1 17.6 us: body(): lax.all_gather(keys, 'ctx', axis=0, tiled=True)]
    ppermute x0 -> x3, waiting for transfers between devices: none -> 21.7 us  [swap(): return lax.ppermute(array, 'ctx', [(i, i ^ r) for i in range(shards)])]
    gather x17 -> x0, other arithmetic: 15.9 us -> none  [the longest x11 11.1 us: body(): key_doc = doc_blocks[piece_key_pos // BLK]]
    dot_general x8 -> x0, matrix products: 10.1 us -> none  [the longest x4 6.07 us: one_block(): jnp.einsum('grqk,kgd->qgrd', probs, value_part, preferred_element_type=jn...]
    ppermute x0 -> x3, starting transfers between devices: none -> 5.62 us  [swap(): return lax.ppermute(array, 'ctx', [(i, i ^ r) for i in range(shards)])]
    reshape x1 -> x0, other arithmetic: 5.59 us -> none  [body(): doc_query_blocks = query_doc.reshape(block_count, query_block)]
    reduce_sum x4 -> x0, other arithmetic: 5.05 us -> none  [one_block(): total = jnp.sum(weight, axis=-1, keepdims=True)]
    pallas_call x0 -> x2, Pallas kernels: none -> 3.75 us  [the longest x1 2.2 us: attend(): pl.pallas_call(lambda *refs: attend_kernel(shards, sources, *refs), in_sp...]
  transfers between devices with their start and end apart: 0 -> 3, of which waited for: 0 -> 2; matrix products, arithmetic and copies ran while one was open for 0% -> 0% of each run, Pallas kernels for 0% -> 0%
where the time goes in v1:
time: 33.7 us; the launch traced here: 33.2 us
  waiting for transfers between devices  21.7 us (64%)
  starting transfers between devices  5.62 us (17%)
  Pallas kernels  3.75 us (11%)
  local copies, waits for them, and re-layouts  1.43 us (4%)
  between operations  0.7 us (2%)
    ppermute x3, waiting for transfers between devices, swap(): return lax.ppermute(array, 'ctx', [(i, i ^ r) for i in range(shards)])  21.7 us
    ppermute x3, starting transfers between devices, swap(): return lax.ppermute(array, 'ctx', [(i, i ^ r) for i in range(shards)])  5.62 us
    pallas_call x1, Pallas kernels, attend(): pl.pallas_call(lambda *refs: attend_kernel(shards, sources, *refs), in_sp...  2.2 us
    pallas_call x1, Pallas kernels, body(): pl.pallas_call(lambda *refs: pack_kernel(shards, *refs), in_specs=[VMEM,...  1.55 us
    unnamed x8, local copies, waits for them, and re-layouts  1.43 us
  transfers between devices with their start and end apart: 3, of which 2 were waited for; matrix products, arithmetic and copies ran while one was open for 0% of the time, Pallas kernels for 0%

profile of v1, /device:TPU:0, one launch (start us, length us, event | category | flops | bytes accessed | tf_op | source)
XLA Modules:
  0.0 33.2 jit_solution(15531155173199971525)
XLA Ops:
  0.0 0.0 copy-start.1
  0.0 0.0 copy-start
  0.0 1.6 %pack.1 = (bf16[1024,128]{1,0:T(8,128)(2,1)S(1)}, bf16[512,128]{1,0:T(8,128)(2,1)S(1)}, bf16[512,128]{1,0:T(8,128)(2,1)S(1)}, bf16[512,128]{1,0:T(8,128)(2,1)S(1)}, s32[1]{0:T(128)}) custom-call(bf16[512,128]{1,0:T(8,128)(2,1)} %refs_0_.1, bf16[512,128]{1,0:T(8,128)(2,1)} %refs_1_.1, s32[16]{0:T(128)} %refs_2_.1), custom_call_target="tpu_custom_call" | custom-call | tf_op jit(solution)/shard_map/pack/pallas_call | solution.py:216
  2.2 0.0 copy-start.3
  2.2 0.0 copy-done.1
  2.2 0.0 copy-done
  2.2 0.6 %copy-done.3 = s32[16]{0:T(128)S(1)} copy-done((s32[16]{0:T(128)S(1)}, s32[16]{0:T(128)}, u32[]{:S(2)}) %copy-start.3) | copy-done | bytes 88
  2.9 29.6 %conditional.1 = (bf16[512,512]{1,0:T(8,128)(2,1)S(1)}) conditional(s32[]{:T(128)} %bitcast, (bf16[512,128]{1,0:T(8,128)(2,1)S(1)}, bf16[512,128]{1,0:T(8,128)(2,1)S(1)}, bf16[512,128]{1,0:T(8,128)(2,1)S(1)}, bf16[512,512]{1,0:T(8,128)(2,1)}, bf16[512,128]{1,0:T(8,128)(2,1)S(1)}, /*index=5*/bf16[512,128]{1,0:T(8,128)(2,1)S(1)}, ...), branch_computations={%region_0.0_spmd, %region_1.0_spmd} | conditional | bytes 3145856 | solution.py:237
  2.9 5.0 %collective-permute-start.5 = (bf16[1024,128]{1,0:T(8,128)(2,1)S(1)}, bf16[1024,128]{1,0:T(8,128)(2,1)S(1)}, u32[]{:S(2)}, u32[]{:S(2)}) collective-permute-start(bf16[1024,128]{1,0:T(8,128)(2,1)S(1)} %get-tuple-element.43), channel_id=1, source_target_pairs={{0,24},{8,16},{16,8},{24,0},{1,25},{9,17},{17,9},{25,1},{2,26},{10... | collective-permute-start | bytes 786440 | tf_op jit(solution)/shard_map/cond/branch_1_fun/ppermute | solution.py:227
  7.9 0.0 collective-permute-start.4
  7.9 0.6 %collective-permute-start.3 = (bf16[1024,128]{1,0:T(8,128)(2,1)S(1)}, bf16[1024,128]{1,0:T(8,128)(2,1)S(1)}, u32[]{:S(2)}, u32[]{:S(2)}) collective-permute-start(bf16[1024,128]{1,0:T(8,128)(2,1)S(1)} %get-tuple-element.43), channel_id=1, source_target_pairs={{0,8},{8,0},{16,24},{24,16},{1,9},{9,1},{17,25},{25,17},{2,10},{10... | collective-permute-start | bytes 786440 | tf_op jit(solution)/shard_map/cond/branch_1_fun/ppermute | solution.py:227
  8.5 6.7 %collective-permute-done.5.refs_6_ = bf16[1024,128]{1,0:T(8,128)(2,1)S(1)} collective-permute-done((bf16[1024,128]{1,0:T(8,128)(2,1)S(1)}, bf16[1024,128]{1,0:T(8,128)(2,1)S(1)}, u32[]{:S(2)}, u32[]{:S(2)}) %collective-permute-start.5) | collective-permute-done | bytes 262176 | tf_op jit(solution)/shard_map/cond/branch_1_fun/ppermute | solution.py:227
  15.2 15.0 %collective-permute-done.4.refs_5_ = bf16[1024,128]{1,0:T(8,128)(2,1)S(1)} collective-permute-done((bf16[1024,128]{1,0:T(8,128)(2,1)S(1)}, bf16[1024,128]{1,0:T(8,128)(2,1)S(1)}, u32[]{:S(2)}, u32[]{:S(2)}) %collective-permute-start.4) | collective-permute-done | bytes 262176 | tf_op jit(solution)/shard_map/cond/branch_1_fun/ppermute | solution.py:227
  30.2 0.0 collective-permute-done.3.refs_4_
  30.2 2.2 %attend.3 = bf16[512,512]{1,0:T(8,128)(2,1)S(1)} custom-call(bf16[512,512]{1,0:T(8,128)(2,1)} %get-tuple-element.39.refs_0_, bf16[512,128]{1,0:T(8,128)(2,1)S(1)} %get-tuple-element.40.refs_1_, bf16[512,128]{1,0:T(8,128)(2,1)S(1)} %get-tuple-element.41.refs_2_, s32[16]{0:T(128)S(1)} %get-tuple-element.42.refs_3_, ...), custom_call_target="tpu_custom_call" | custom-call | tf_op jit(solution)/shard_map/cond/branch_1_fun/attend/pallas_call | solution.py:199
  32.4 0.0 copy-start.2
  32.5 0.8 %copy-done.2 = bf16[512,512]{1,0:T(8,128)(2,1)} copy-done((bf16[512,512]{1,0:T(8,128)(2,1)}, bf16[512,512]{1,0:T(8,128)(2,1)S(1)}, u32[]{:S(2)}) %copy-start.2) | copy-done | bytes 524312
Async XLA Ops:
  0.0 2.2 %copy-start.1 = (bf16[512,128]{1,0:T(8,128)(2,1)S(1)}, bf16[512,128]{1,0:T(8,128)(2,1)}, u32[]{:S(2)}) copy-start(bf16[512,128]{1,0:T(8,128)(2,1)} %refs_1_.1) | copy-start | bytes 393220
  0.0 2.2 %copy-start = (bf16[512,128]{1,0:T(8,128)(2,1)S(1)}, bf16[512,128]{1,0:T(8,128)(2,1)}, u32[]{:S(2)}) copy-start(bf16[512,128]{1,0:T(8,128)(2,1)} %refs_0_.1) | copy-start | bytes 393220
  2.2 0.7 %copy-start.3 = (s32[16]{0:T(128)S(1)}, s32[16]{0:T(128)}, u32[]{:S(2)}) copy-start(s32[16]{0:T(128)} %refs_2_.1) | copy-start | bytes 196
  2.9 12.3 %collective-permute-start.5 = (bf16[1024,128]{1,0:T(8,128)(2,1)S(1)}, bf16[1024,128]{1,0:T(8,128)(2,1)S(1)}, u32[]{:S(2)}, u32[]{:S(2)}) collective-permute-start(bf16[1024,128]{1,0:T(8,128)(2,1)S(1)} %get-tuple-element.43), channel_id=1, source_target_pairs={{0,24},{8,16},{16,8},{24,0},{1,25},{9,17},{17,9},{25,1},{2,26},{10... | collective-permute-start | bytes 786440 | tf_op jit(solution)/shard_map/cond/branch_1_fun/ppermute | solution.py:227
  7.9 22.3 %collective-permute-start.4 = (bf16[1024,128]{1,0:T(8,128)(2,1)S(1)}, bf16[1024,128]{1,0:T(8,128)(2,1)S(1)}, u32[]{:S(2)}, u32[]{:S(2)}) collective-permute-start(bf16[1024,128]{1,0:T(8,128)(2,1)S(1)} %get-tuple-element.43), channel_id=1, source_target_pairs={{0,16},{8,24},{16,0},{24,8},{1,17},{9,25},{17,1},{25,9},{2,18},{10... | collective-permute-start | bytes 786440 | tf_op jit(solution)/shard_map/cond/branch_1_fun/ppermute | solution.py:227
  7.9 22.3 %collective-permute-start.3 = (bf16[1024,128]{1,0:T(8,128)(2,1)S(1)}, bf16[1024,128]{1,0:T(8,128)(2,1)S(1)}, u32[]{:S(2)}, u32[]{:S(2)}) collective-permute-start(bf16[1024,128]{1,0:T(8,128)(2,1)S(1)} %get-tuple-element.43), channel_id=1, source_target_pairs={{0,8},{8,0},{16,24},{24,16},{1,9},{9,1},{17,25},{25,17},{2,10},{10... | collective-permute-start | bytes 786440 | tf_op jit(solution)/shard_map/cond/branch_1_fun/ppermute | solution.py:227
  32.4 0.8 %copy-start.2 = (bf16[512,512]{1,0:T(8,128)(2,1)}, bf16[512,512]{1,0:T(8,128)(2,1)S(1)}, u32[]{:S(2)}) copy-start(bf16[512,512]{1,0:T(8,128)(2,1)S(1)} %get-tuple-element.63) | copy-start | bytes 1572868

commit v2 on v0

v2 whole, which is shorter than its diff:
```python
import math

import jax
import jax.numpy as jnp
from jax import lax
from jax.experimental import pallas as pl
from jax.experimental.pallas import tpu as pltpu
from jax.sharding import PartitionSpec as P

HD = 128
BLK = 128
MASKED = -1e30
SCALE2 = HD ** (-0.5) * math.log2(math.e)
VMEM = pl.BlockSpec(memory_space=pltpu.VMEM)
SMEM = pl.BlockSpec(memory_space=pltpu.SMEM)


ANY = pl.BlockSpec(memory_space=pl.ANY)


def normalised(mixed):
    inverse = pl.reciprocal(mixed[:, HD:], approx=True)
    inverse = inverse * (2.0 - mixed[:, HD:] * inverse)
    return (mixed[:, :HD] * inverse).astype(jnp.bfloat16)


class Tiles:
    def __init__(self, shards, span, heads, q_ref, doc_ref, m_ref, acc_ref):
        self.span, self.heads = span, heads
        self.q_ref, self.doc_ref, self.m_ref, self.acc_ref = q_ref, doc_ref, m_ref, acc_ref
        self.me = lax.axis_index("ctx")
        self.per_span = span // BLK
        self.chunk = min(span, 2 * BLK)
        self.blocks = self.chunk // BLK
        self.chunks = span // self.chunk
        self.spans = (self.me, 2 * shards - 1 - self.me)
        row_in = lax.broadcasted_iota(jnp.int32, (BLK, BLK), 0)
        col_in = lax.broadcasted_iota(jnp.int32, (BLK, BLK), 1)
        self.triangle = jnp.where(col_in <= row_in, 0.0, MASKED).astype(jnp.float32)

    def query_block(self, t, query_chunk):
        return self.spans[t] * self.per_span + query_chunk * self.blocks

    def tile(self, t, query_chunk, source, key_block, key_blocks, diagonal=False, o_ref=None):
        keys, key_row, values, value_row = source
        key_rows = pl.ds(pl.multiple_of(key_row, BLK), key_blocks * BLK)
        value_rows = pl.ds(pl.multiple_of(value_row, BLK), key_blocks * BLK)
        rows = pl.ds(pl.multiple_of(t * self.span + query_chunk * self.chunk, BLK), self.chunk)
        query_block = self.query_block(t, query_chunk)
        bias = {}
        for a in range(self.blocks):
            for c in range(key_blocks):
                same = self.doc_ref[query_block + a] == self.doc_ref[key_block + c]
                if diagonal and c > a:
                    same = jnp.bool_(False)
                bias[a, c] = jnp.where(same, 0.0, MASKED).astype(jnp.float32)
        key = keys[key_rows, :]
        ones = jnp.ones((key_blocks * BLK, HD), jnp.bfloat16)
        value = jnp.concatenate([values[value_rows, :], ones], axis=1)
        for h in range(self.heads):
            query = self.q_ref[rows, h * HD : (h + 1) * HD]
            scores = lax.dot_general(
                query, key, (((1,), (1,)), ((), ())), preferred_element_type=jnp.float32
            )
            lines, peaks = [], []
            for a in range(self.blocks):
                line = []
                for c in range(key_blocks):
                    part = scores[a * BLK : (a + 1) * BLK, c * BLK : (c + 1) * BLK]
                    part = part + bias[a, c]
                    if diagonal and a == c:
                        part = part + self.triangle
                    line.append(part)
                top = line[0]
                for part in line[1:]:
                    top = jnp.maximum(top, part)
                peaks.append(jnp.broadcast_to(jnp.max(top, axis=1, keepdims=True), (BLK, HD)))
                lines.append(line)
            peak = jnp.concatenate(peaks, axis=0)
            if not diagonal:
                before = self.m_ref[h, rows, :]
                peak = jnp.maximum(peak, before)
            weights = jnp.concatenate(
                [
                    jnp.concatenate(
                        [
                            jnp.exp2((part - peak[a * BLK : (a + 1) * BLK]) * SCALE2)
                            for part in line
                        ],
                        axis=1,
                    )
                    for a, line in enumerate(lines)
                ],
                axis=0,
            ).astype(jnp.bfloat16)
            mixed = jnp.dot(weights, value, preferred_element_type=jnp.float32)
            if not diagonal:
                shrink = jnp.exp2((before - peak) * SCALE2)
                mixed = mixed + self.acc_ref[h, rows, :] * jnp.concatenate([shrink, shrink], axis=1)
            if o_ref is None:
                self.m_ref[h, rows, :] = peak
                self.acc_ref[h, rows, :] = mixed
            else:
                o_ref[rows, h * HD : (h + 1) * HD] = normalised(mixed)

    def reaches(self, t, query_chunk, key_block, key_blocks):
        last = self.doc_ref[key_block + key_blocks - 1]
        return last == self.doc_ref[self.query_block(t, query_chunk)]

    def earlier(self, t, query_chunk, source, key_block, key_blocks, valid=True):
        @pl.when(self.reaches(t, query_chunk, key_block, key_blocks) & valid)
        def _():
            self.tile(t, query_chunk, source, key_block, key_blocks)

    def whole_span(self, t, source, key_span, valid=True):
        keys, key_row, values, value_row = source

        def step(index, carry):
            query_chunk, key_chunk = index // self.chunks, index % self.chunks
            row = key_chunk * self.chunk
            self.earlier(
                t,
                query_chunk,
                (keys, key_row + row, values, value_row + row),
                key_span * self.per_span + key_chunk * self.blocks,
                self.blocks,
                valid,
            )
            return carry

        if self.chunks == 1:
            step(0, 0)
        else:
            lax.fori_loop(0, self.chunks * self.chunks, step, 0)

    def local(self, own, key_row, value_row):
        for t in range(2):

            def step(index, carry, t=t):
                def source(chunk):
                    row = t * self.span + chunk * self.chunk
                    return own, key_row + row, own, value_row + row

                self.tile(
                    t, index, source(index), self.query_block(t, index), self.blocks, diagonal=True
                )

                def before(key_chunk, inner):
                    key_block = self.query_block(t, key_chunk)
                    self.earlier(t, index, source(key_chunk), key_block, self.blocks)
                    return inner

                if self.chunks > 1:
                    lax.fori_loop(0, index, before, 0)
                return carry

            if self.chunks == 1:
                step(0, 0)
            else:
                lax.fori_loop(0, self.chunks, step, 0)
        self.whole_span(1, (own, key_row, own, value_row), self.spans[0])

    def finish(self, t, o_ref):
        rows = pl.ds(t * self.span, self.span)
        for h in range(self.heads):
            o_ref[rows, h * HD : (h + 1) * HD] = normalised(self.acc_ref[h, rows, :])


def gathered_kernel(shards, q_ref, own, doc_ref, all_k, all_v, o_ref, m_ref, acc_ref):
    span, heads = q_ref.shape[0] // 2, q_ref.shape[1] // HD
    tiles = Tiles(shards, span, heads, q_ref, doc_ref, m_ref, acc_ref)
    tiles.local(own, 0, 2 * span)
    for t in range(2):

        def span_step(s, carry, t=t):
            holder = jnp.minimum(s, 2 * shards - 1 - s)
            row = (2 * holder + jnp.where(s < shards, 0, 1)) * span
            other = (s != tiles.spans[0]) if t == 1 else True
            tiles.whole_span(t, (all_k, row, all_v, row), s, other)
            return carry

        lax.fori_loop(0, tiles.spans[t], span_step, 0)
        tiles.finish(t, o_ref)


def partner_span(tiles, shards, r):
    partner = tiles.me ^ r
    return jnp.where(partner < tiles.me, partner, 2 * shards - 1 - partner)


def crosses(doc_ref, per_span):
    return doc_ref[4 * per_span - 1] == doc_ref[6 * per_span]


def reads_last(tiles, shards, t):
    key_span = partner_span(tiles, shards, 3)
    reaches = tiles.reaches(t, 0, key_span * tiles.per_span, tiles.blocks)
    return reaches & (key_span < tiles.spans[t])


def local_kernel(shards, q_hbm, own, doc_ref, q_ref, m_ref, acc_ref, sem):
    heads = q_ref.shape[1] // HD
    span = q_ref.shape[0] // 2
    fetch = pltpu.make_async_copy(q_hbm, q_ref, sem)
    fetch.start()
    fetch.wait()
    Tiles(shards, span, heads, q_ref, doc_ref, m_ref, acc_ref).local(own, 0, 2 * span)


def middle_kernel(shards, q_ref, doc_ref, m_in, acc_in, from2, from1, fix1, fix0, *refs):
    m_ref, acc_ref, o_ref = refs
    heads = q_ref.shape[1] // HD
    span = q_ref.shape[0] // 2
    half = span // 2
    before = Tiles(shards, span, heads, q_ref, doc_ref, m_in, acc_in)
    tiles = Tiles(shards, span, heads, q_ref, doc_ref, m_ref, acc_ref)
    me, per_span, blocks = tiles.me, tiles.per_span, tiles.blocks
    for t in range(2):
        sources = []
        for r, ref in ((2, from2), (1, from1)):
            key_span = partner_span(tiles, shards, r)
            source = (ref, 0, ref, span)
            sources.append((source, key_span * per_span, blocks, key_span < tiles.spans[t]))
        if t == 1:
            half_blocks = half // BLK
            block = jnp.where(me == 0, 3, 2) * per_span + per_span - half_blocks
            middle = (me == 1) | (me == 2)
            sources.append(((fix1, 0, fix1, span), 3 * per_span, blocks, middle))
            sources.append(((fix0, 0, fix0, half), block, half_blocks, me < 2))
        reads = [tiles.reaches(t, 0, block, count) & valid for _, block, count, valid in sources]
        more = reads_last(tiles, shards, t)
        changes = more
        for read in reads:
            changes = changes | read

        @pl.when(changes)
        def _(t=t):
            rows = pl.ds(t * span, span)
            m_ref[:, rows, :] = m_in[:, rows, :]
            acc_ref[:, rows, :] = acc_in[:, rows, :]

        for read, (source, block, count, _) in zip(reads, sources):

            @pl.when(read)
            def _(t=t, source=source, block=block, count=count):
                tiles.tile(t, 0, source, block, count)

        @pl.when(changes & jnp.logical_not(more))
        def _(t=t):
            tiles.finish(t, o_ref)

        @pl.when(jnp.logical_not(changes))
        def _(t=t):
            before.finish(t, o_ref)


def last_kernel(shards, q_ref, doc_ref, m_ref, acc_ref, part_ref, from3, o_hbm, o_ref, sems):
    heads = q_ref.shape[1] // HD
    span = q_ref.shape[0] // 2
    tiles = Tiles(shards, span, heads, q_ref, doc_ref, m_ref, acc_ref)
    key_block = partner_span(tiles, shards, 3) * tiles.per_span
    reads = [reads_last(tiles, shards, t) for t in range(2)]

    def copy(t, source):
        rows = pl.ds(t * span, span)
        return pltpu.make_async_copy(source.at[rows], o_hbm.at[rows], sems.at[t])

    for t in range(2):

        @pl.when(jnp.logical_not(reads[t]))
        def _(t=t):
            copy(t, part_ref).start()

    for t in range(2):

        @pl.when(reads[t])
        def _(t=t):
            tiles.tile(t, 0, (from3, 0, from3, span), key_block, tiles.blocks, o_ref=o_ref)
            copy(t, o_ref).start()

    for t in range(2):
        copy(t, o_ref).wait()


def plan_kernel(doc_ref, plan_ref):
    per_span = doc_ref.shape[0] // 8
    beside = doc_ref[4 * per_span - 1] == doc_ref[5 * per_span]
    plan_ref[0] = jnp.where(crosses(doc_ref, per_span), 2, jnp.where(beside, 1, 0))


def body(queries, keys, values, doc_blocks):
    shards = lax.axis_size("ctx")
    rows, heads = queries.shape[0], queries.shape[1] // HD
    span = rows // 2
    params = pltpu.CompilerParams(vmem_limit_bytes=16 * 1024 * 1024)
    state_shapes = [
        jax.ShapeDtypeStruct((heads, rows, HD), jnp.float32),
        jax.ShapeDtypeStruct((heads, rows, 2 * HD), jnp.float32),
    ]
    state_scratch = [pltpu.VMEM(x.shape, x.dtype) for x in state_shapes]
    out_shape = jax.ShapeDtypeStruct(queries.shape, jnp.bfloat16)

    if shards != 4:
        received = [lax.all_gather(x, "ctx", axis=0, tiled=True) for x in (keys, values)]
        return pl.pallas_call(
            lambda *refs: gathered_kernel(shards, *refs),
            in_specs=[VMEM, VMEM, SMEM, VMEM, VMEM],
            out_specs=VMEM,
            out_shape=out_shape,
            scratch_shapes=state_scratch,
            compiler_params=params,
            name="attend",
        )(queries, jnp.concatenate([keys, values]), doc_blocks, *received)

    me = lax.axis_index("ctx")

    def swap(array, r):
        return lax.ppermute(array, "ctx", [(i, i ^ r) for i in range(shards)])

    def send(array, *pairs):
        return lax.ppermute(array, "ctx", pairs)

    own = lax.optimization_barrier(jnp.concatenate([keys, values], axis=0))

    def span_for(r, own):
        row = jnp.where((me ^ r) > me, 0, span)
        parts = [lax.dynamic_slice_in_dim(own, row + base, span, 0) for base in (0, rows)]
        return jnp.concatenate(parts, axis=0)

    def lower_rows(start):
        return jnp.concatenate([own[start:span], own[rows + start : rows + span]], axis=0)

    far = span_for(2, own)
    far, own = lax.optimization_barrier((far, own))
    near, lower, half = span_for(1, own), lower_rows(0), lower_rows(span // 2)
    from2, from1, from3 = swap(far, 2), swap(near, 1), swap(far, 3)
    plan = pl.pallas_call(
        plan_kernel,
        in_specs=[SMEM],
        out_specs=SMEM,
        out_shape=jax.ShapeDtypeStruct((1,), jnp.int32),
        name="plan",
    )(doc_blocks)

    def narrow(lower, half):
        return lower, half

    def beside(lower, half):
        return send(lower, (3, 2)), half

    def crossing(lower, half):
        fix1, fix0 = send(lower, (3, 1)), send(half, (3, 0), (2, 1))
        return fix1 + send(lower, (3, 2)), fix0

    fixes = lax.switch(plan[0], [narrow, beside, crossing], lower, half)
    q, m, acc = pl.pallas_call(
        lambda *refs: local_kernel(shards, *refs),
        in_specs=[ANY, VMEM, SMEM],
        out_specs=[VMEM] * 3,
        out_shape=[out_shape] + state_shapes,
        scratch_shapes=[pltpu.SemaphoreType.DMA],
        compiler_params=params,
        name="local",
    )(queries, own, doc_blocks)
    m, acc, part = pl.pallas_call(
        lambda *refs: middle_kernel(shards, *refs),
        in_specs=[VMEM, SMEM] + [VMEM] * 6,
        out_specs=[VMEM] * 3,
        out_shape=state_shapes + [out_shape],
        compiler_params=params,
        name="middle",
    )(q, doc_blocks, m, acc, from2, from1, *fixes)
    return pl.pallas_call(
        lambda *refs: last_kernel(shards, *refs),
        in_specs=[VMEM, SMEM] + [VMEM] * 4,
        out_specs=ANY,
        out_shape=out_shape,
        scratch_shapes=[
            pltpu.VMEM(out_shape.shape, out_shape.dtype),
            pltpu.SemaphoreType.DMA((2,)),
        ],
        compiler_params=params,
        name="last",
    )(q, doc_blocks, m, acc, part, from3)


def solution(mesh):
    return jax.shard_map(
        body,
        mesh=mesh,
        in_specs=(P("ctx", "tp"), P("ctx", "tp"), P("ctx", "tp"), P()),
        out_specs=P("ctx", "tp"),
        check_vma=False,
    )
```

time: 77.3 us -> 18.1 us (0.23)
  the two profiles are of different devices: /device:TPU:0 before, /device:TPU:17 now
where the time goes in v2:
time: 18.1 us; the launch traced here: 17.9 us
  waiting for transfers between devices  7 us (39%)
  Pallas kernels  6.17 us (34%)
  starting transfers between devices  2.82 us (16%)
  other arithmetic  1.08 us (6%)
  between operations  0.75 us (4%)
    ppermute x3, waiting for transfers between devices, swap(): return lax.ppermute(array, 'ctx', [(i, i ^ r) for i in range(shards)])  7 us
    ppermute x3, starting transfers between devices, swap(): return lax.ppermute(array, 'ctx', [(i, i ^ r) for i in range(shards)])  2.82 us
    pallas_call x1, Pallas kernels, body(): pl.pallas_call(lambda *refs: last_kernel(shards, *refs), in_specs=[VMEM,...  1.99 us
    pallas_call x1, Pallas kernels, body(): pl.pallas_call(lambda *refs: middle_kernel(shards, *refs), in_specs=[VMEM...  1.5 us
    pallas_call x1, Pallas kernels, body(): pl.pallas_call(lambda *refs: local_kernel(shards, *refs), in_specs=[ANY,...  1.5 us
    pallas_call x1, Pallas kernels, body(): pl.pallas_call(plan_kernel, in_specs=[SMEM], out_specs=SMEM, out_shape=ja...  1.19 us
    concatenate x1, other arithmetic, body(): own = lax.optimization_barrier(jnp.concatenate([keys, values], axis=0))  1.04 us
  transfers between devices with their start and end apart: 3, of which 2 were waited for; matrix products, arithmetic and copies ran while one was open for 0% of the time, Pallas kernels for 23%

profile of v2, /device:TPU:17, one launch (start us, length us, event | category | flops | bytes accessed | tf_op | source)
XLA Modules:
  0.0 17.9 jit_solution(7428149888077236164)
XLA Ops:
  0.0 0.0 copy-start.1
  0.0 0.0 copy-start
  0.0 1.0 %pad_maximum_fusion.refs_1_ = bf16[1024,128]{1,0:T(8,128)(2,1)S(1)} fusion(bf16[512,128]{1,0:T(8,128)(2,1)} %param.9, bf16[512,128]{1,0:T(8,128)(2,1)} %param.8), kind=kLoop, calls=%fused_computation | loop fusion | flops 524288 | bytes 524288 | tf_op jit(solution)/shard_map/concatenate | solution.py:323
  1.1 0.1 collective-permute-start.4
  1.2 1.4 %collective-permute-start.5 = (bf16[512,128]{1,0:T(8,128)(2,1)S(1)}, bf16[512,128]{1,0:T(8,128)(2,1)S(1)}, u32[]{:S(2)}, u32[]{:S(2)}) collective-permute-start(bf16[512,128]{1,0:T(8,128)(2,1)S(1)} %pad_maximum_fusion.2), channel_id=1, source_target_pairs={{0,8},{8,0},{16,24},{24,16},{1,9},{9,1},{17,25},{25,17},{2,10},{10... | collective-permute-start | bytes 393224 | tf_op jit(solution)/shard_map/ppermute | solution.py:318
  2.7 1.2 %plan.1 = s32[1]{0:T(128)} custom-call(s32[16]{0:T(128)} %refs_1_.3), custom_call_target="tpu_custom_call" | custom-call | tf_op jit(solution)/shard_map/plan/pallas_call | solution.py:337
  4.5 1.4 %collective-permute-start.6 = (bf16[512,128]{1,0:T(8,128)(2,1)S(1)}, bf16[512,128]{1,0:T(8,128)(2,1)S(1)}, u32[]{:S(2)}, u32[]{:S(2)}) collective-permute-start(bf16[512,128]{1,0:T(8,128)(2,1)S(1)} %pad_maximum_fusion.1), channel_id=1, source_target_pairs={{0,24},{8,16},{16,8},{24,0},{1,25},{9,17},{17,9},{25,1},{2,26},{10... | collective-permute-start | bytes 393224 | tf_op jit(solution)/shard_map/ppermute | solution.py:318
  5.9 0.0 copy-done.1
  5.9 0.0 copy-done
  5.9 1.5 %local.1 = (bf16[512,512]{1,0:T(8,128)(2,1)S(1)}, f32[4,512,128]{2,1,0:T(8,128)S(1)}, f32[4,512,256]{2,1,0:T(8,128)S(1)}) custom-call(bf16[512,512]{1,0:T(8,128)(2,1)S(1)} %copy-done, bf16[1024,128]{1,0:T(8,128)(2,1)S(1)} %pad_maximum_fusion.refs_1_, s32[16]{0:T(128)S(1)} %copy-done.1), custom_call_target="tpu_custom_call" | custom-call | tf_op jit(solution)/shard_map/local/pallas_call | solution.py:356
  7.4 0.0 collective-permute-done.4.refs_4_
  7.4 0.9 %collective-permute-done.5.refs_5_ = bf16[512,128]{1,0:T(8,128)(2,1)S(1)} collective-permute-done((bf16[512,128]{1,0:T(8,128)(2,1)S(1)}, bf16[512,128]{1,0:T(8,128)(2,1)S(1)}, u32[]{:S(2)}, u32[]{:S(2)}) %collective-permute-start.5) | collective-permute-done | bytes 131104 | tf_op jit(solution)/shard_map/ppermute | solution.py:318
  8.3 1.5 %middle.1 = (f32[4,512,128]{2,1,0:T(8,128)S(1)}, f32[4,512,256]{2,1,0:T(8,128)S(1)}, bf16[512,512]{1,0:T(8,128)(2,1)S(1)}) custom-call(bf16[512,512]{1,0:T(8,128)(2,1)S(1)} %get-tuple-element.32.refs_0_, s32[16]{0:T(128)S(1)} %copy-done.1, f32[4,512,128]{2,1,0:T(8,128)S(1)} %get-tuple-element.33.refs_2_, f32[4,512,256]{2,1,0:T(8,128)S(1)} %get-tuple-element.34.refs_3_, ...), custom_call_target="tpu_custom_call" | custom-call | tf_op jit(solution)/shard_map/middle/pallas_call | solution.py:365
  9.8 6.1 %collective-permute-done.6.refs_5_ = bf16[512,128]{1,0:T(8,128)(2,1)S(1)} collective-permute-done((bf16[512,128]{1,0:T(8,128)(2,1)S(1)}, bf16[512,128]{1,0:T(8,128)(2,1)S(1)}, u32[]{:S(2)}, u32[]{:S(2)}) %collective-permute-start.6) | collective-permute-done | bytes 131104 | tf_op jit(solution)/shard_map/ppermute | solution.py:318
  15.9 2.0 %last.1 = bf16[512,512]{1,0:T(8,128)(2,1)} custom-call(bf16[512,512]{1,0:T(8,128)(2,1)S(1)} %get-tuple-element.32.refs_0_, s32[16]{0:T(128)S(1)} %copy-done.1, f32[4,512,128]{2,1,0:T(8,128)S(1)} %get-tuple-element.38.refs_2_, f32[4,512,256]{2,1,0:T(8,128)S(1)} %get-tuple-element.39.refs_3_, bf16[512,512]{1,0:T(8,128)(2,1)S(1)} %get-tuple-element.40.refs_4_, ...), custom_call_target="tpu_custom_call" | custom-call | tf_op jit(solution)/shard_map/last/pallas_call | solution.py:373
  (8 shorter events, 0.1 us)
Async XLA Ops:
  0.0 5.9 %copy-start.1 = (s32[16]{0:T(128)S(1)}, s32[16]{0:T(128)}, u32[]{:S(2)}) copy-start(s32[16]{0:T(128)} %refs_1_.3) | copy-start | bytes 196
  0.0 5.9 %copy-start = (bf16[512,512]{1,0:T(8,128)(2,1)S(1)}, bf16[512,512]{1,0:T(8,128)(2,1)}, u32[]{:S(2)}) copy-start(bf16[512,512]{1,0:T(8,128)(2,1)} %refs_0_.1) | copy-start | bytes 1572868
  1.1 6.3 %collective-permute-start.4 = (bf16[512,128]{1,0:T(8,128)(2,1)S(1)}, bf16[512,128]{1,0:T(8,128)(2,1)S(1)}, u32[]{:S(2)}, u32[]{:S(2)}) collective-permute-start(bf16[512,128]{1,0:T(8,128)(2,1)S(1)} %pad_maximum_fusion.1), channel_id=1, source_target_pairs={{0,16},{8,24},{16,0},{24,8},{1,17},{9,25},{17,1},{25,9},{2,18},{10... | collective-permute-start | bytes 393224 | tf_op jit(solution)/shard_map/ppermute | solution.py:318
  1.2 7.1 %collective-permute-start.5 = (bf16[512,128]{1,0:T(8,128)(2,1)S(1)}, bf16[512,128]{1,0:T(8,128)(2,1)S(1)}, u32[]{:S(2)}, u32[]{:S(2)}) collective-permute-start(bf16[512,128]{1,0:T(8,128)(2,1)S(1)} %pad_maximum_fusion.2), channel_id=1, source_target_pairs={{0,8},{8,0},{16,24},{24,16},{1,9},{9,1},{17,25},{25,17},{2,10},{10... | collective-permute-start | bytes 393224 | tf_op jit(solution)/shard_map/ppermute | solution.py:318
  4.5 11.4 %collective-permute-start.6 = (bf16[512,128]{1,0:T(8,128)(2,1)S(1)}, bf16[512,128]{1,0:T(8,128)(2,1)S(1)}, u32[]{:S(2)}, u32[]{:S(2)}) collective-permute-start(bf16[512,128]{1,0:T(8,128)(2,1)S(1)} %pad_maximum_fusion.1), channel_id=1, source_target_pairs={{0,24},{8,16},{16,8},{24,0},{1,25},{9,17},{17,9},{25,1},{2,26},{10... | collective-permute-start | bytes 393224 | tf_op jit(solution)/shard_map/ppermute | solution.py:318
